TPU v7x, 32 devices: a whole 2x2x4 slice. The times are simulated.
32 devices in a mesh: req: 16 (over z, y, x), tp: 2 (over core).
Axes of the slice: x: 2, y: 2, z: 4, core: 2. Of those that a mesh axis runs over, the one named last changes fastest.
Arguments:
- residual: bfloat16 [512, 2048], P('req'), may hold values from -6 to 6
- fresh_qkv: bfloat16 [512, 3, 2048], P('req', None, 'tp'), may hold values from -32 to 32
- kv_cache: bfloat16 [512, 24, 2, 2048], P('req', None, None, 'tp'), may hold values from -32 to 32
- cache_len: int32 [512], P('req'), may hold values from 2 to 24, as said below
- out_proj: bfloat16 [2048, 2048], P('tp'), may hold values from -0.125 to 0.125
- norm_gain: float32 [2048], replicated, may hold values from 0.1 to 1.9
- router_weight: float32 [2048, 16], replicated, may hold values from -7.9549513 to 7.9549513
- expert_ids: int32 [512, 8], P('req'), may hold values from 0 to 15, all different within a row; in each aligned block of 32 rows (0 to 31, 32 to 63, ...) at most 32 rows name the same one
- gate_up: bfloat16 [16, 2048, 2, 1024], P('req', None, None, 'tp'), may hold values from -0.125 to 0.125
- down_proj: bfloat16 [16, 1024, 2048], P('req', 'tp'), may hold values from -0.1875 to 0.1875
Outputs:
- layer_out: bfloat16 [512, 2048], P('req', 'tp')
Inputs may be any that keep to these rules, and one draw needn't show every extreme that they name: `expert_ids`: each row names 8 different experts; among the 32 rows of one device no expert is named by more than 32 rows, and some device reaches 32. `cache_len`: some request uses all 24 positions.
All inputs are finite; a program needn't handle non-finite values.
Results may differ from a plain program's by a relative error of at most 0.018.
Values may be sent and summed in bfloat16 or wider, within the bound.
A program may use at most 128 MiB of HBM per device.

v0:
```python
import jax
import jax.numpy as jnp
from jax import lax
from jax.sharding import PartitionSpec as P

HD = 128


def rms_normed(hidden_in, gain):
    values = hidden_in.astype(jnp.float32)
    scale_inv = lax.rsqrt(jnp.mean(values * values, axis=-1, keepdims=True) + 1e-05)
    return (values * scale_inv * gain).astype(jnp.bfloat16)


def attend(fresh_qkv, kv_cache, cache_len):
    requests, ctx_len = (kv_cache.shape[0], kv_cache.shape[1])
    local_heads = fresh_qkv.shape[2] // HD
    queries = fresh_qkv[:, 0].reshape(requests, local_heads, HD)
    new_keys = fresh_qkv[:, 1].reshape(requests, local_heads, HD)
    new_values = fresh_qkv[:, 2].reshape(requests, local_heads, HD)
    cache_keys = kv_cache[:, :, 0].reshape(requests, ctx_len, local_heads, HD)
    cache_values = kv_cache[:, :, 1].reshape(requests, ctx_len, local_heads, HD)
    factor = HD ** (-0.5)
    scores = (
        jnp.einsum("nhd,nchd->nhc", queries, cache_keys, preferred_element_type=jnp.float32)
        * factor
    )
    own_score = (
        jnp.einsum("nhd,nhd->nh", queries, new_keys, preferred_element_type=jnp.float32) * factor
    )
    valid = (jnp.arange(ctx_len, dtype=jnp.int32)[None, :] < cache_len[:, None])[:, None, :]
    masked = jnp.where(valid, scores, -jnp.inf)
    top_score = jnp.maximum(jnp.max(masked, axis=-1), own_score)
    expos = jnp.where(valid, jnp.exp(masked - top_score[..., None]), 0.0)
    own_expo = jnp.exp(own_score - top_score)
    total = jnp.sum(expos, axis=-1) + own_expo
    weights = (expos / total[..., None]).astype(jnp.bfloat16)
    own_weight = (own_expo / total).astype(jnp.bfloat16)
    mixed = jnp.einsum("nhc,nchd->nhd", weights, cache_values, preferred_element_type=jnp.float32)
    mixed = mixed + own_weight.astype(jnp.float32)[..., None] * new_values.astype(jnp.float32)
    return mixed.astype(jnp.bfloat16).reshape(requests, local_heads * HD)


def local(
    residual,
    fresh_qkv,
    kv_cache,
    cache_len,
    out_proj,
    norm_gain,
    router_weight,
    expert_ids,
    gate_up,
    down_proj,
):
    tp_place = lax.axis_index("tp")
    me = lax.axis_index("req")
    experts = lax.axis_size("req")
    attended = attend(fresh_qkv, kv_cache, cache_len)
    partial_value = jnp.dot(attended, out_proj, preferred_element_type=jnp.float32)
    summed = lax.psum(partial_value, "tp")
    hidden = (residual.astype(jnp.float32) + summed).astype(jnp.bfloat16)
    normed = rms_normed(hidden, norm_gain)
    rows = lax.all_gather(normed, "req", axis=0, tiled=True)
    logits = jnp.dot(normed.astype(jnp.float32), router_weight, precision=lax.Precision.HIGHEST)
    named = jnp.any(
        expert_ids[:, :, None] == jnp.arange(experts, dtype=jnp.int32)[None, None, :], axis=1
    )
    gates = jax.nn.softmax(jnp.where(named, logits, -jnp.inf), axis=-1)
    gates_all = lax.all_gather(gates, "req", axis=0, tiled=True)
    mine = jnp.arange(experts, dtype=jnp.int32)[None, :] == me
    weight = jnp.sum(jnp.where(mine, gates_all, 0.0), axis=1, keepdims=True)
    gate_part = jnp.dot(rows, gate_up[0, :, 0], preferred_element_type=jnp.float32)
    up_part = jnp.dot(rows, gate_up[0, :, 1], preferred_element_type=jnp.float32)
    inner = (jax.nn.silu(gate_part) * up_part).astype(jnp.bfloat16)
    result = jnp.dot(inner, down_proj[0], preferred_element_type=jnp.float32)
    own = lax.psum_scatter(result * weight, "tp", scatter_dimension=1, tiled=True)
    moe_share = lax.psum_scatter(own, "req", scatter_dimension=0, tiled=True)
    width_here = moe_share.shape[1]
    own_cols = lax.dynamic_slice_in_dim(hidden, tp_place * width_here, width_here, 1)
    return (own_cols.astype(jnp.float32) + moe_share).astype(jnp.bfloat16)


def solution(mesh):
    in_specs = (
        P("req", None),
        P("req", None, "tp"),
        P("req", None, None, "tp"),
        P("req"),
        P("tp", None),
        P(),
        P(),
        P("req", None),
        P("req", None, None, "tp"),
        P("req", "tp", None),
    )
    out_specs = P("req", "tp")
    return jax.shard_map(local, mesh=mesh, in_specs=in_specs, out_specs=out_specs, check_vma=False)
```

profile of v0, /device:TPU:0, one launch (start us, length us, event | category | flops | bytes accessed | tf_op | source)
XLA Modules:
  0.0 234.0 jit_solution(13227113264910571109)
XLA Ops:
  6.5 0.8 iota_compare_fusion.1
  7.4 0.9 convert_bitcast_fusion
  8.4 0.1 fusion.20
  8.5 0.1 copy.30
  8.5 0.1 reshape.54
  8.6 17.1 %slice_reduce_fusion = (bf16[32,24,1024]{2,1,0:T(8,128)(2,1)}, bf16[32,24,1024]{2,1,0:T(8,128)(2,1)S(1)}) fusion(bf16[32,24,2,1024]{3,2,1,0:T(2,128)(2,1)} %param.12), kind=kLoop, calls=%fused_computation.1 | loop fusion | bytes 6291456 | tf_op jit(solution)/shard_map/slice | solution.py:22
  25.7 0.9 fusion.6
  26.7 0.1 copy.26
  26.9 0.1 copy.20
  27.0 0.2 copy.31
  27.2 2.0 fusion.3
  29.2 0.1 fusion.19
  29.3 3.8 %fusion.24 = f32[32,2048]{1,0:T(8,128)} fusion(bf16[1024,2048]{1,0:T(8,128)(2,1)} %param.14, bf16[4,8,8,128]{3,2,1,0:T(8,128)(2,1)S(1)} %bitcast.84), kind=kOutput, calls=%fused_computation.40 | convolution fusion | flops 134217728 | bytes 4521984 | tf_op jit(solution)/shard_map/dot_general | solution.py:60
  33.1 0.0 all-reduce.2.cloned.1.call-update
  33.1 0.0 all-gather.3.cloned.1.call-start
  33.2 21.1 %all-reduce.2.cloned.1.call-done = f32[32,2048]{1,0:T(8,128)} async-done(((f32[32,2048]{1,0:T(8,128)}), f32[32,2048]{1,0:T(8,128)}) %all-reduce.2.cloned.1.call-update) | async-done | bytes 262160 | tf_op jit(solution)/shard_map/psum | solution.py:61
  54.3 1.1 fusion.15
  55.4 0.7 fusion.17
  56.1 0.0 all-gather.3.cloned.1.call-update
  56.1 0.0 reduce-scatter.3.cloned.1.call-start
  56.3 10.4 %fusion.33 = (bf16[1,2048,1,512]{3,2,1,0:T(2,128)(2,1)}, bf16[1,2048,1,512]{3,2,1,0:T(2,128)(2,1)}) fusion(bf16[1,2048,2,512]{3,2,1,0:T(2,128)(2,1)} %param.18), kind=kLoop, calls=%fused_computation.61 | loop fusion | bytes 8388608 | tf_op jit(solution)/shard_map/slice | solution.py:73
  66.7 0.2 fusion.34
  67.0 41.8 %all-gather = f32[16,32,16]{1,2,0:T(8,128)S(1)} all-gather(f32[1,32,16]{1,2,0:T(8,128)S(1)} %divide_bitcast_fusion), channel_id=1, replica_groups=mesh['req'=16,'tp'=2] {'req'}, dimensions={0}, use_global_device_ids=true | all-gather | bytes 34816 | tf_op jit(solution)/shard_map/all_gather | solution.py:70
  108.9 0.1 reshape.46
  109.0 0.1 select_reduce_fusion
  109.1 10.6 %all-gather.3.cloned.1.call-done = bf16[512,2048]{1,0:T(8,128)(2,1)} async-done(((bf16[32,2048]{1,0:T(8,128)(2,1)}), bf16[512,2048]{1,0:T(8,128)(2,1)}) %all-gather.3.cloned.1.call-update) | async-done | bytes 2097168 | tf_op jit(solution)/shard_map/all_gather | solution.py:64
  119.6 4.1 %fusion.1 = f32[512,512]{1,0:T(8,128)S(1)} fusion(bf16[512,2048]{1,0:T(8,128)(2,1)} %all-gather.3.cloned.1.call-done, bf16[1,2048,1,512]{3,2,1,0:T(2,128)(2,1)} %get-tuple-element.9), kind=kOutput, calls=%fused_computation.6 | convolution fusion | flops 1073741824 | bytes 5242880 | tf_op jit(solution)/shard_map/dot_general | solution.py:73
  123.7 7.3 %convolution_multiply_fusion = f32[512,2048]{1,0:T(8,128)} fusion(bf16[1,512,2048]{2,1,0:T(8,128)(2,1)S(1)} %copy-done, f32[512]{0:T(512)S(1)} %select_reduce_fusion, bf16[512,2048]{1,0:T(8,128)(2,1)} %all-gather.3.cloned.1.call-done, bf16[1,2048,1,512]{3,2,1,0:T(2,128)(2,1)} %get-tuple-element.10, f32[512,512]{1,0:T(8,128)S(1)} %fusion.1), kind=kOutput, calls=%fused_computation | convolution fusion | flops 2150105088 | bytes 11536384 | tf_op jit(solution)/shard_map/dot_general | solution.py:76
  131.0 0.0 reduce-scatter.5.cloned.1.call-start
  131.1 10.8 %reduce-scatter.3.cloned.1.call-done = f32[512,1024]{1,0:T(8,128)} async-done(((f32[512,2048]{1,0:T(8,128)}), f32[512,1024]{1,0:T(8,128)}) %reduce-scatter.3.cloned.1.call-update) | async-done | bytes 2097168 | tf_op jit(solution)/shard_map/reduce_scatter | solution.py:77
  141.9 84.1 %reduce-scatter.5.cloned.1.call-done = f32[32,1024]{1,0:T(8,128)} async-done(((f32[512,1024]{1,0:T(8,128)}), f32[32,1024]{1,0:T(8,128)}) %reduce-scatter.5.cloned.1.call-update) | async-done | bytes 131088 | tf_op jit(solution)/shard_map/reduce_scatter | solution.py:78
  226.0 1.5 add_convert_fusion.1
  (29 shorter events, 0.4 us)
Async XLA Ops:
  6.5 117.2 %copy-start = (bf16[1,512,2048]{2,1,0:T(8,128)(2,1)S(1)}, bf16[1,512,2048]{2,1,0:T(8,128)(2,1)}, u32[]{:S(2)}) copy-start(bf16[1,512,2048]{2,1,0:T(8,128)(2,1)} %param.19) | copy-start | bytes 6291460
  6.5 47.7 %all-reduce.2.cloned.1.call-start = ((), (), s32[]{:S(2)}) async-start(), calls=%async_computation.2 | async-start | bytes 524288 | tf_op jit(solution)/shard_map/psum | solution.py:61
  29.3 25.0 %copy-start.2 = (bf16[32,2048]{1,0:T(8,128)(2,1)S(1)}, bf16[32,2048]{1,0:T(8,128)(2,1)}, u32[]{:S(2)}) copy-start(bf16[32,2048]{1,0:T(8,128)(2,1)} %param.10) | copy-start | bytes 393220
  29.3 26.1 %copy-start.4 = (f32[2048]{0:T(1024)S(1)}, f32[2048]{0:T(1024)}, u32[]{:S(2)}) copy-start(f32[2048]{0:T(1024)} %param.15) | copy-start | bytes 24580
  29.3 26.9 %copy-start.5 = (s32[32,8]{0,1:T(8,128)S(1)}, s32[32,8]{0,1:T(8,128)}, u32[]{:S(2)}) copy-start(s32[32,8]{0,1:T(8,128)} %param.17) | copy-start | bytes 3076
  33.1 86.5 %all-gather.3.cloned.1.call-start = ((), (), s32[]{:S(2)}) async-start(), calls=%async_computation.3 | async-start | bytes 2228224 | tf_op jit(solution)/shard_map/all_gather | solution.py:64
  56.1 85.7 %reduce-scatter.3.cloned.1.call-start = ((), (), s32[]{:S(2)}) async-start(), calls=%async_computation.4 | async-start | bytes 6291456 | tf_op jit(solution)/shard_map/reduce_scatter | solution.py:77
  56.2 10.5 %copy-start.1 = (bf16[32,2048]{1,0:T(8,128)(2,1)S(1)}, bf16[32,2048]{1,0:T(8,128)(2,1)}, u32[]{:S(2)}) copy-start(bf16[32,2048]{1,0:T(8,128)(2,1)} %fusion.17) | copy-start | bytes 393220
  56.3 10.5 %copy-start.3 = (f32[2048,16]{0,1:T(8,128)S(1)}, f32[2048,16]{0,1:T(8,128)}, u32[]{:S(2)}) copy-start(f32[2048,16]{0,1:T(8,128)} %param.16) | copy-start | bytes 393220
  131.0 95.0 %reduce-scatter.5.cloned.1.call-start = ((), (), s32[]{:S(2)}) async-start(), calls=%async_computation.5 | async-start | bytes 2228224 | tf_op jit(solution)/shard_map/reduce_scatter | solution.py:78
Sparse Core Ops, SparseCore 0:
  33.3 20.9 all-reduce.1
  57.4 62.1 all-gather.2
  131.1 10.6 reduce-scatter.2
  144.0 81.9 reduce-scatter.4
where the time goes:
time: 234 us
  waiting for transfers between devices  127 us (54%)
  blocking collectives  41.8 us (18%)
  local copies, waits for them, and re-layouts  28.3 us (12%)
  matrix products  18.2 us (8%)
  between operations  13.3 us (6%)
  other arithmetic  5.64 us (2%)
    reduce_scatter x1, waiting for transfers between devices, local(): moe_share = lax.psum_scatter(own, 'req', scatter_dimension=0, tiled=True)  84.1 us
    all_gather x1, blocking collectives, local(): gates_all = lax.all_gather(gates, 'req', axis=0, tiled=True)  41.8 us
    psum x1, waiting for transfers between devices, local(): summed = lax.psum(partial_value, 'tp')  21.1 us
    slice x1, local copies, waits for them, and re-layouts, attend(): cache_values = kv_cache[:, :, 1].reshape(requests, ctx_len, local_heads, HD)  17.1 us
    reduce_scatter x1, waiting for transfers between devices, local(): lax.psum_scatter(result * weight, 'tp', scatter_dimension=1, tiled=True)  10.8 us
    all_gather x1, waiting for transfers between devices, local(): rows = lax.all_gather(normed, 'req', axis=0, tiled=True)  10.6 us
    slice x1, local copies, waits for them, and re-layouts, local(): gate_up[0, :, 0]  10.4 us
    dot_general x1, matrix products, local(): result = jnp.dot(inner, down_proj[0], preferred_element_type=jnp.float32)  7.25 us
  transfers between devices with their start and end apart: 4, of which 4 were waited for; matrix products, arithmetic and copies ran while one was open for 5% of the time, Pallas kernels for 0%

commit v1 on v0

--- a/solution.py
+++ b/solution.py
@@ -61,7 +61,15 @@
     summed = lax.psum(partial_value, "tp")
     hidden = (residual.astype(jnp.float32) + summed).astype(jnp.bfloat16)
     normed = rms_normed(hidden, norm_gain)
-    rows = lax.all_gather(normed, "req", axis=0, tiled=True)
+    ways, here = (lax.axis_size("req"), lax.axis_index("req"))
+    grown, reach = (normed, 1)
+    while reach < ways:
+        theirs = lax.ppermute(grown, "req", [(d, d ^ reach) for d in range(ways)])
+        mine_first = jnp.concatenate([grown, theirs], axis=0)
+        theirs_first = jnp.concatenate([theirs, grown], axis=0)
+        grown = jnp.where(here & reach == 0, mine_first, theirs_first)
+        reach = 2 * reach
+    rows = grown
     logits = jnp.dot(normed.astype(jnp.float32), router_weight, precision=lax.Precision.HIGHEST)
     named = jnp.any(
         expert_ids[:, :, None] == jnp.arange(experts, dtype=jnp.int32)[None, None, :], axis=1

time: 234 us -> 275 us (1.18)
  waiting for transfers between devices: 127 us -> 144 us
  blocking collectives: 41.8 us -> 51.5 us
  starting transfers between devices: 0.13 us -> 8.17 us
  matrix products: 18.2 us -> 21.1 us
    ppermute x0 -> x4, waiting for transfers between devices: none -> 20.7 us  [local(): theirs = lax.ppermute(grown, 'req', [(d, d ^ reach) for d in range(ways)])]
    all_gather x1 -> x0, waiting for transfers between devices: 10.6 us -> none  [local(): rows = lax.all_gather(normed, 'req', axis=0, tiled=True)]
    all_gather x1, blocking collectives: 41.8 us -> 51.5 us  [local(): gates_all = lax.all_gather(gates, 'req', axis=0, tiled=True)]
    ppermute x0 -> x4, starting transfers between devices: none -> 8.08 us  [local(): theirs = lax.ppermute(grown, 'req', [(d, d ^ reach) for d in range(ways)])]
    reduce_scatter x1, waiting for transfers between devices: 10.8 us -> 18.4 us  [local(): lax.psum_scatter(result * weight, 'tp', scatter_dimension=1, tiled=True)]
    select_n x0 -> x3, other arithmetic: none -> 2.78 us  [local(): grown = jnp.where(here & reach == 0, mine_first, theirs_first)]
  transfers between devices with their start and end apart: 4 -> 7, of which waited for: 4 -> 6; matrix products, arithmetic and copies ran while one was open for 5% -> 4% of each run, Pallas kernels for 0% -> 0%
where the time goes in v1:
time: 275 us; the launch traced here: 274 us
  waiting for transfers between devices  144 us (52%)
  blocking collectives  51.5 us (19%)
  local copies, waits for them, and re-layouts  28.2 us (10%)
  matrix products  21.1 us (8%)
  between operations  13.3 us (5%)
  starting transfers between devices  8.17 us (3%)
  other arithmetic  7.77 us (3%)
    reduce_scatter x1, waiting for transfers between devices, local(): moe_share = lax.psum_scatter(own, 'req', scatter_dimension=0, tiled=True)  84.1 us
    all_gather x1, blocking collectives, local(): gates_all = lax.all_gather(gates, 'req', axis=0, tiled=True)  51.5 us
    psum x1, waiting for transfers between devices, local(): summed = lax.psum(partial_value, 'tp')  21.1 us
    ppermute x4, waiting for transfers between devices, local(): theirs = lax.ppermute(grown, 'req', [(d, d ^ reach) for d in range(ways)])  20.7 us
    reduce_scatter x1, waiting for transfers between devices, local(): lax.psum_scatter(result * weight, 'tp', scatter_dimension=1, tiled=True)  18.4 us
    slice x1, local copies, waits for them, and re-layouts, attend(): cache_values = kv_cache[:, :, 1].reshape(requests, ctx_len, local_heads, HD)  17.1 us
    slice x1, local copies, waits for them, and re-layouts, local(): gate_up[0, :, 0]  10.4 us
    dot_general x1, matrix products, local(): result = jnp.dot(inner, down_proj[0], preferred_element_type=jnp.float32)  8.36 us
  transfers between devices with their start and end apart: 7, of which 6 were waited for; matrix products, arithmetic and copies ran while one was open for 4% of the time, Pallas kernels for 0%

profile of v1, /device:TPU:0, one launch (start us, length us, event | category | flops | bytes accessed | tf_op | source)
XLA Modules:
  0.0 274.5 jit_solution(7646172629015376529)
XLA Ops:
  6.5 0.8 iota_compare_fusion.1
  7.4 0.9 convert_bitcast_fusion
  8.4 0.1 fusion.15
  8.6 17.1 %slice_reduce_fusion = (bf16[32,24,1024]{2,1,0:T(8,128)(2,1)}, bf16[32,24,1024]{2,1,0:T(8,128)(2,1)S(1)}) fusion(bf16[32,24,2,1024]{3,2,1,0:T(2,128)(2,1)} %param.12), kind=kLoop, calls=%fused_computation.1 | loop fusion | bytes 6291456 | tf_op jit(solution)/shard_map/slice | solution.py:22
  25.7 0.9 fusion.6
  26.7 0.1 copy.26
  27.0 0.2 copy.31
  27.2 2.0 fusion.3
  29.2 0.1 fusion.14
  29.3 3.8 %fusion.19 = f32[32,2048]{1,0:T(8,128)} fusion(bf16[1024,2048]{1,0:T(8,128)(2,1)} %param.14, bf16[4,8,8,128]{3,2,1,0:T(8,128)(2,1)S(1)} %bitcast.80), kind=kOutput, calls=%fused_computation.40 | convolution fusion | flops 134217728 | bytes 4521984 | tf_op jit(solution)/shard_map/dot_general | solution.py:60
  33.1 21.1 %all-reduce.2.cloned.1.call-done = f32[32,2048]{1,0:T(8,128)} async-done(((f32[32,2048]{1,0:T(8,128)}), f32[32,2048]{1,0:T(8,128)}) %all-reduce.2.cloned.1.call-update) | async-done | bytes 262160 | tf_op jit(solution)/shard_map/psum | solution.py:61
  54.2 1.1 fusion.10
  55.3 0.1 fusion.12
  55.4 1.8 collective-permute-start
  57.2 4.0 %collective-permute-done = bf16[32,2048]{1,0:T(8,128)(2,1)S(1)} collective-permute-done((bf16[32,2048]{1,0:T(8,128)(2,1)S(1)}, bf16[32,2048]{1,0:T(8,128)(2,1)S(1)}, u32[]{:S(2)}, u32[]{:S(2)}) %collective-permute-start) | collective-permute-done | bytes 131104 | tf_op jit(solution)/shard_map/ppermute | solution.py:67
  61.2 1.8 collective-permute-start.1
  63.1 6.0 %collective-permute-done.1 = bf16[64,2048]{1,0:T(8,128)(2,1)S(1)} collective-permute-done((bf16[64,2048]{1,0:T(8,128)(2,1)S(1)}, bf16[64,2048]{1,0:T(8,128)(2,1)S(1)}, u32[]{:S(2)}, u32[]{:S(2)}) %collective-permute-start.1) | collective-permute-done | bytes 262176 | tf_op jit(solution)/shard_map/ppermute | solution.py:67
  69.0 0.1 maximum_select_fusion.2
  69.1 1.8 collective-permute-start.2
  70.9 10.8 %collective-permute-done.2 = bf16[128,2048]{1,0:T(8,128)(2,1)} collective-permute-done((bf16[128,2048]{1,0:T(8,128)(2,1)S(1)}, bf16[128,2048]{1,0:T(8,128)(2,1)}, u32[]{:S(2)}, u32[]{:S(2)}) %collective-permute-start.2) | collective-permute-done | bytes 524320 | tf_op jit(solution)/shard_map/ppermute | solution.py:67
  81.7 2.6 maximum_select_fusion.1
  84.3 2.7 collective-permute-start.3
  87.0 10.4 %fusion.31 = (bf16[1,2048,1,512]{3,2,1,0:T(2,128)(2,1)}, bf16[1,2048,1,512]{3,2,1,0:T(2,128)(2,1)}) fusion(bf16[1,2048,2,512]{3,2,1,0:T(2,128)(2,1)} %param.18), kind=kLoop, calls=%fused_computation.63 | loop fusion | bytes 8388608 | tf_op jit(solution)/shard_map/slice | solution.py:81
  97.5 0.2 fusion.32
  97.7 51.5 %all-gather = f32[16,32,16]{1,2,0:T(8,128)S(1)} all-gather(f32[1,32,16]{1,2,0:T(8,128)S(1)} %divide_bitcast_fusion), channel_id=1, replica_groups=mesh['req'=16,'tp'=2] {'req'}, dimensions={0}, use_global_device_ids=true | all-gather | bytes 34816 | tf_op jit(solution)/shard_map/all_gather | solution.py:78
  149.3 0.1 reshape.46
  149.4 0.1 select_reduce_fusion
  149.5 5.9 %fusion = f32[512,512]{1,0:T(8,128)} fusion(bf16[1,2048,1,512]{3,2,1,0:T(2,128)(2,1)} %get-tuple-element.10, bf16[256,2048]{1,0:T(8,128)(2,1)} %collective-permute-done.3, bf16[256,2048]{1,0:T(8,128)(2,1)} %maximum_select_fusion.1, pred[]{:T(512)S(6)} %eq.36), kind=kOutput, calls=%fused_computation.5 | convolution fusion | flops 1083179008 | bytes 5242881 | tf_op jit(solution)/shard_map/dot_general | solution.py:82
  155.4 8.4 %convolution_multiply_fusion = f32[512,2048]{1,0:T(8,128)} fusion(bf16[1,512,2048]{2,1,0:T(8,128)(2,1)S(1)} %copy-done, f32[512]{0:T(512)S(1)} %select_reduce_fusion, f32[512,512]{1,0:T(8,128)} %fusion, bf16[1,2048,1,512]{3,2,1,0:T(2,128)(2,1)} %get-tuple-element.9, bf16[256,2048]{1,0:T(8,128)(2,1)} %collective-permute-done.3, ...), kind=kOutput, calls=%fused_computation | convolution fusion | flops 2159542272 | bytes 11536385 | tf_op jit(solution)/shard_map/dot_general | solution.py:84
  163.8 18.4 %reduce-scatter.3.cloned.1.call-done = f32[512,1024]{1,0:T(8,128)} async-done(((f32[512,2048]{1,0:T(8,128)}), f32[512,1024]{1,0:T(8,128)}) %reduce-scatter.3.cloned.1.call-update) | async-done | bytes 2097168 | tf_op jit(solution)/shard_map/reduce_scatter | solution.py:85
  182.3 84.1 %reduce-scatter.5.cloned.1.call-done = f32[32,1024]{1,0:T(8,128)} async-done(((f32[512,1024]{1,0:T(8,128)}), f32[32,1024]{1,0:T(8,128)}) %reduce-scatter.5.cloned.1.call-update) | async-done | bytes 131088 | tf_op jit(solution)/shard_map/reduce_scatter | solution.py:86
  266.4 1.5 add_convert_fusion.1
  (35 shorter events, 0.7 us)
Async XLA Ops:
  6.5 148.8 %copy-start = (bf16[1,512,2048]{2,1,0:T(8,128)(2,1)S(1)}, bf16[1,512,2048]{2,1,0:T(8,128)(2,1)}, u32[]{:S(2)}) copy-start(bf16[1,512,2048]{2,1,0:T(8,128)(2,1)} %param.19) | copy-start | bytes 6291460
  6.5 47.7 %all-reduce.2.cloned.1.call-start = ((), (), s32[]{:S(2)}) async-start(), calls=%async_computation.2 | async-start | bytes 524288 | tf_op jit(solution)/shard_map/psum | solution.py:61
  29.3 24.9 %copy-start.1 = (bf16[32,2048]{1,0:T(8,128)(2,1)S(1)}, bf16[32,2048]{1,0:T(8,128)(2,1)}, u32[]{:S(2)}) copy-start(bf16[32,2048]{1,0:T(8,128)(2,1)} %param.10) | copy-start | bytes 393220
  29.3 26.0 %copy-start.3 = (f32[2048]{0:T(1024)S(1)}, f32[2048]{0:T(1024)}, u32[]{:S(2)}) copy-start(f32[2048]{0:T(1024)} %param.15) | copy-start | bytes 24580
  33.1 149.1 %reduce-scatter.3.cloned.1.call-start = ((), (), s32[]{:S(2)}) async-start(), calls=%async_computation.3 | async-start | bytes 6291456 | tf_op jit(solution)/shard_map/reduce_scatter | solution.py:85
  55.4 5.8 %collective-permute-start = (bf16[32,2048]{1,0:T(8,128)(2,1)S(1)}, bf16[32,2048]{1,0:T(8,128)(2,1)S(1)}, u32[]{:S(2)}, u32[]{:S(2)}) collective-permute-start(bf16[32,2048]{1,0:T(8,128)(2,1)S(1)} %fusion.12), channel_id=1, source_target_pairs={{0,2},{2,0},{4,6},{6,4},{8,10},{10,8},{12,14},{14,12},{16,18},{18,... | collective-permute-start | bytes 393224 | tf_op jit(solution)/shard_map/ppermute | solution.py:67
  61.2 7.8 %collective-permute-start.1 = (bf16[64,2048]{1,0:T(8,128)(2,1)S(1)}, bf16[64,2048]{1,0:T(8,128)(2,1)S(1)}, u32[]{:S(2)}, u32[]{:S(2)}) collective-permute-start(bf16[64,2048]{1,0:T(8,128)(2,1)S(1)} %maximum_select_fusion.6), channel_id=1, source_target_pairs={{0,4},{2,6},{4,0},{6,2},{8,12},{10,14},{12,8},{14,10},{16,20},{18,... | collective-permute-start | bytes 786440 | tf_op jit(solution)/shard_map/ppermute | solution.py:67
  69.1 12.6 %collective-permute-start.2 = (bf16[128,2048]{1,0:T(8,128)(2,1)S(1)}, bf16[128,2048]{1,0:T(8,128)(2,1)}, u32[]{:S(2)}, u32[]{:S(2)}) collective-permute-start(bf16[128,2048]{1,0:T(8,128)(2,1)S(1)} %maximum_select_fusion.2), channel_id=1, source_target_pairs={{0,8},{2,10},{4,12},{6,14},{8,0},{10,2},{12,4},{14,6},{16,24},{18,... | collective-permute-start | bytes 1572872 | tf_op jit(solution)/shard_map/ppermute | solution.py:67
  84.3 13.1 %copy-start.4 = (s32[32,8]{0,1:T(8,128)S(1)}, s32[32,8]{0,1:T(8,128)}, u32[]{:S(2)}) copy-start(s32[32,8]{0,1:T(8,128)} %param.17) | copy-start | bytes 3076
  84.3 13.1 %copy-start.2 = (f32[2048,16]{0,1:T(8,128)S(1)}, f32[2048,16]{0,1:T(8,128)}, u32[]{:S(2)}) copy-start(f32[2048,16]{0,1:T(8,128)} %param.16) | copy-start | bytes 393220
  84.3 65.1 %collective-permute-start.3 = (bf16[256,2048]{1,0:T(8,128)(2,1)}, bf16[256,2048]{1,0:T(8,128)(2,1)}, u32[]{:S(2)}, u32[]{:S(2)}) collective-permute-start(bf16[256,2048]{1,0:T(8,128)(2,1)} %maximum_select_fusion.1), channel_id=1, source_target_pairs={{0,16},{2,18},{4,20},{6,22},{8,24},{10,26},{12,28},{14,30},{16,0},... | collective-permute-start | bytes 3145736 | tf_op jit(solution)/shard_map/ppermute | solution.py:67
  163.7 102.7 %reduce-scatter.5.cloned.1.call-start = ((), (), s32[]{:S(2)}) async-start(), calls=%async_computation.4 | async-start | bytes 2228224 | tf_op jit(solution)/shard_map/reduce_scatter | solution.py:86
Sparse Core Ops, SparseCore 0:
  33.2 20.9 all-reduce.1
  163.9 18.3 reduce-scatter.2
  184.5 81.8 reduce-scatter.4
